TPU v7x, 32 devices: a whole 2x2x4 slice. The times are simulated.
32 devices in a mesh: groups: 2 (over x), blk: 16 (over z, y, core).
Axes of the slice: x: 2, y: 2, z: 4, core: 2. Of those that a mesh axis runs over, the one named last changes fastest.
Arguments:
- points: bfloat16 [16384, 256], P(('groups', 'blk')), parts along dimension 0, may hold values from -6 to 6
- left_vec: bfloat16 [16384, 64], P(('groups', 'blk')), parts along dimension 0, may hold values from -6 to 6
- right_vec: bfloat16 [16384, 64], P(('groups', 'blk')), parts along dimension 0, may hold values from -6 to 6
Outputs:
- kernel_vu: float32 [16384, 128], P(('groups', 'blk')), parts along dimension 0
- feature_grad: float32 [16384, 256], P(('groups', 'blk')), parts along dimension 0
There are 2 independent parts, one for each index of `groups`. A program takes and returns all parts, laid end to end along the dimension named above; each array names one. Nothing has to cross between parts.
All inputs are finite; a program needn't handle non-finite values.
Results may differ from a plain program's by a relative error of at most 0.0031.
Values may be sent and summed in bfloat16 or wider, within the bound.
A program may use at most 64 MiB of HBM per device.

v0:
```python
import math

import jax
import jax.numpy as jnp
from jax import lax
from jax.sharding import PartitionSpec as P


def from_behind(array, axis, by):
    peers = lax.axis_size(axis)
    return lax.ppermute(array, axis, [(i, (i + by) % peers) for i in range(peers)])


def pair_terms(own_x, own_left, far_x, far_right):
    width = own_x.shape[1]
    gram = lax.dot_general(
        own_x, far_x, (((1,), (1,)), ((), ())), preferred_element_type=jnp.float32
    )
    own_sq = jnp.sum(jnp.square(own_x.astype(jnp.float32)), axis=1)
    far_sq = jnp.sum(jnp.square(far_x.astype(jnp.float32)), axis=1)
    kernel = jnp.exp(-(own_sq[:, None] + far_sq[None, :] - 2.0 * gram) / width)
    kernel_bf = kernel.astype(jnp.bfloat16)
    inner = lax.dot_general(
        own_left, far_right, (((1,), (1,)), ((), ())), preferred_element_type=jnp.float32
    )
    mixed = kernel * inner
    mixed_bf = mixed.astype(jnp.bfloat16)
    near_vu = jnp.dot(kernel_bf, far_right, preferred_element_type=jnp.float32)
    near_grad = jnp.dot(mixed_bf, far_x, preferred_element_type=jnp.float32) - jnp.sum(
        mixed, axis=1
    )[:, None] * own_x.astype(jnp.float32)
    return (near_vu, near_grad)


def per_device(points, left_vec, right_vec):
    count = lax.axis_size("blk")
    rows = points.shape[0]
    own_left = jnp.concatenate([left_vec, right_vec], axis=1)
    own_right = jnp.concatenate([right_vec, left_vec], axis=1)
    self_vu, self_grad = pair_terms(points, own_left, points, own_right)

    def visit(turn_index, state_now):
        far_x, far_right, total_vu, total_grad = state_now
        far_x, far_right = from_behind((far_x, far_right), "blk", 1)
        near_vu, near_grad = pair_terms(points, own_left, far_x, far_right)
        return (far_x, far_right, total_vu + near_vu, total_grad + near_grad)

    final_state = lax.fori_loop(1, count, visit, (points, own_right, self_vu, self_grad))
    total_vu, total_grad = (final_state[2], final_state[3])
    scale = 1.0 / math.sqrt(rows * count)
    return (total_vu * scale, total_grad * scale)


def solution(mesh):
    return jax.shard_map(
        per_device,
        mesh=mesh,
        in_specs=(
            P(("groups", "blk"), None),
            P(("groups", "blk"), None),
            P(("groups", "blk"), None),
        ),
        out_specs=(P(("groups", "blk"), None), P(("groups", "blk"), None)),
        check_vma=False,
    )
```

profile of v0, /device:TPU:0, one launch (start us, length us, event | category | flops | bytes accessed | tf_op | source)
XLA Modules:
  0.0 184.5 jit_solution(13226653231257471019)
XLA Ops:
  0.6 1.1 fusion.13
  1.9 0.7 copy-done.2
  2.9 0.8 copy-done
  5.1 177.8 %while.16 = (s32[]{:T(128)}, bf16[512,256]{1,0:T(8,128)(2,1)S(1)}, bf16[512,128]{1,0:T(8,128)(2,1)S(1)}, f32[512,128]{1,0:T(8,128)S(1)}, f32[512,256]{1,0:T(8,12...) while((s32[]{:T(128)}, bf16[512,256]{1,0:T(8,128)(2,1)S(1)}, ...), condition=%wide.region_6.7_spmd, body=%wide.region_2.6_spmd.sunk | while | flops 407435776 | bytes 10109093 | solution.py:48
  5.6 2.6 %collective-permute-start.1 = (bf16[512,128]{1,0:T(8,128)(2,1)S(1)}, bf16[512,128]{1,0:T(8,128)(2,1)S(1)}, u32[]{:S(2)}, u32[]{:S(2)}) collective-permute-start(bf16[512,128]{1,0:T(8,128)(2,1)S(1)} %get-tuple-element.123), channel_id=1, source_target_pairs={{0,1},{1,2},{2,3},{3,4},{4,5},{5,6},{6,7},{7,8},{8,9},{9,10},{10,1... | collective-permute-start | bytes 393224 | tf_op jit(solution)/shard_map/while/body/eval_jaxpr/ppermute | solution.py:11
  8.4 7.7 %collective-permute-done.1 = bf16[512,128]{1,0:T(8,128)(2,1)S(1)} collective-permute-done((bf16[512,128]{1,0:T(8,128)(2,1)S(1)}, bf16[512,128]{1,0:T(8,128)(2,1)S(1)}, u32[]{:S(2)}, u32[]{:S(2)}) %collective-permute-start.1) | collective-permute-done | bytes 131104 | tf_op jit(solution)/shard_map/while/body/eval_jaxpr/ppermute | solution.py:11
  18.2 9.7 %collective-permute-done.1 = bf16[512,128]{1,0:T(8,128)(2,1)S(1)} collective-permute-done((bf16[512,128]{1,0:T(8,128)(2,1)S(1)}, bf16[512,128]{1,0:T(8,128)(2,1)S(1)}, u32[]{:S(2)}, u32[]{:S(2)}) %collective-permute-start.1) | collective-permute-done | bytes 131104 | tf_op jit(solution)/shard_map/while/body/eval_jaxpr/ppermute | solution.py:11
  28.4 0.5 convolution_add_fusion.2
  30.0 9.7 %collective-permute-done.1 = bf16[512,128]{1,0:T(8,128)(2,1)S(1)} collective-permute-done((bf16[512,128]{1,0:T(8,128)(2,1)S(1)}, bf16[512,128]{1,0:T(8,128)(2,1)S(1)}, u32[]{:S(2)}, u32[]{:S(2)}) %collective-permute-start.1) | collective-permute-done | bytes 131104 | tf_op jit(solution)/shard_map/while/body/eval_jaxpr/ppermute | solution.py:11
  41.8 9.7 %collective-permute-done.1 = bf16[512,128]{1,0:T(8,128)(2,1)S(1)} collective-permute-done((bf16[512,128]{1,0:T(8,128)(2,1)S(1)}, bf16[512,128]{1,0:T(8,128)(2,1)S(1)}, u32[]{:S(2)}, u32[]{:S(2)}) %collective-permute-start.1) | collective-permute-done | bytes 131104 | tf_op jit(solution)/shard_map/while/body/eval_jaxpr/ppermute | solution.py:11
  52.0 0.5 convolution_add_fusion.2
  53.6 9.7 %collective-permute-done.1 = bf16[512,128]{1,0:T(8,128)(2,1)S(1)} collective-permute-done((bf16[512,128]{1,0:T(8,128)(2,1)S(1)}, bf16[512,128]{1,0:T(8,128)(2,1)S(1)}, u32[]{:S(2)}, u32[]{:S(2)}) %collective-permute-start.1) | collective-permute-done | bytes 131104 | tf_op jit(solution)/shard_map/while/body/eval_jaxpr/ppermute | solution.py:11
  65.4 9.7 %collective-permute-done.1 = bf16[512,128]{1,0:T(8,128)(2,1)S(1)} collective-permute-done((bf16[512,128]{1,0:T(8,128)(2,1)S(1)}, bf16[512,128]{1,0:T(8,128)(2,1)S(1)}, u32[]{:S(2)}, u32[]{:S(2)}) %collective-permute-start.1) | collective-permute-done | bytes 131104 | tf_op jit(solution)/shard_map/while/body/eval_jaxpr/ppermute | solution.py:11
  77.1 9.7 %collective-permute-done.1 = bf16[512,128]{1,0:T(8,128)(2,1)S(1)} collective-permute-done((bf16[512,128]{1,0:T(8,128)(2,1)S(1)}, bf16[512,128]{1,0:T(8,128)(2,1)S(1)}, u32[]{:S(2)}, u32[]{:S(2)}) %collective-permute-start.1) | collective-permute-done | bytes 131104 | tf_op jit(solution)/shard_map/while/body/eval_jaxpr/ppermute | solution.py:11
  88.9 9.7 %collective-permute-done.1 = bf16[512,128]{1,0:T(8,128)(2,1)S(1)} collective-permute-done((bf16[512,128]{1,0:T(8,128)(2,1)S(1)}, bf16[512,128]{1,0:T(8,128)(2,1)S(1)}, u32[]{:S(2)}, u32[]{:S(2)}) %collective-permute-start.1) | collective-permute-done | bytes 131104 | tf_op jit(solution)/shard_map/while/body/eval_jaxpr/ppermute | solution.py:11
  100.7 9.7 %collective-permute-done.1 = bf16[512,128]{1,0:T(8,128)(2,1)S(1)} collective-permute-done((bf16[512,128]{1,0:T(8,128)(2,1)S(1)}, bf16[512,128]{1,0:T(8,128)(2,1)S(1)}, u32[]{:S(2)}, u32[]{:S(2)}) %collective-permute-start.1) | collective-permute-done | bytes 131104 | tf_op jit(solution)/shard_map/while/body/eval_jaxpr/ppermute | solution.py:11
  112.5 9.7 %collective-permute-done.1 = bf16[512,128]{1,0:T(8,128)(2,1)S(1)} collective-permute-done((bf16[512,128]{1,0:T(8,128)(2,1)S(1)}, bf16[512,128]{1,0:T(8,128)(2,1)S(1)}, u32[]{:S(2)}, u32[]{:S(2)}) %collective-permute-start.1) | collective-permute-done | bytes 131104 | tf_op jit(solution)/shard_map/while/body/eval_jaxpr/ppermute | solution.py:11
  124.3 9.7 %collective-permute-done.1 = bf16[512,128]{1,0:T(8,128)(2,1)S(1)} collective-permute-done((bf16[512,128]{1,0:T(8,128)(2,1)S(1)}, bf16[512,128]{1,0:T(8,128)(2,1)S(1)}, u32[]{:S(2)}, u32[]{:S(2)}) %collective-permute-start.1) | collective-permute-done | bytes 131104 | tf_op jit(solution)/shard_map/while/body/eval_jaxpr/ppermute | solution.py:11
  136.1 9.7 %collective-permute-done.1 = bf16[512,128]{1,0:T(8,128)(2,1)S(1)} collective-permute-done((bf16[512,128]{1,0:T(8,128)(2,1)S(1)}, bf16[512,128]{1,0:T(8,128)(2,1)S(1)}, u32[]{:S(2)}, u32[]{:S(2)}) %collective-permute-start.1) | collective-permute-done | bytes 131104 | tf_op jit(solution)/shard_map/while/body/eval_jaxpr/ppermute | solution.py:11
  147.9 9.7 %collective-permute-done.1 = bf16[512,128]{1,0:T(8,128)(2,1)S(1)} collective-permute-done((bf16[512,128]{1,0:T(8,128)(2,1)S(1)}, bf16[512,128]{1,0:T(8,128)(2,1)S(1)}, u32[]{:S(2)}, u32[]{:S(2)}) %collective-permute-start.1) | collective-permute-done | bytes 131104 | tf_op jit(solution)/shard_map/while/body/eval_jaxpr/ppermute | solution.py:11
  159.6 9.7 %collective-permute-done.1 = bf16[512,128]{1,0:T(8,128)(2,1)S(1)} collective-permute-done((bf16[512,128]{1,0:T(8,128)(2,1)S(1)}, bf16[512,128]{1,0:T(8,128)(2,1)S(1)}, u32[]{:S(2)}, u32[]{:S(2)}) %collective-permute-start.1) | collective-permute-done | bytes 131104 | tf_op jit(solution)/shard_map/while/body/eval_jaxpr/ppermute | solution.py:11
  171.4 9.7 %collective-permute-done.1 = bf16[512,128]{1,0:T(8,128)(2,1)S(1)} collective-permute-done((bf16[512,128]{1,0:T(8,128)(2,1)S(1)}, bf16[512,128]{1,0:T(8,128)(2,1)S(1)}, u32[]{:S(2)}, u32[]{:S(2)}) %collective-permute-start.1) | collective-permute-done | bytes 131104 | tf_op jit(solution)/shard_map/while/body/eval_jaxpr/ppermute | solution.py:11
  182.9 0.8 broadcast_multiply_fusion
  183.8 0.7 broadcast_multiply_fusion.1
  (174 shorter events, 31.7 us)
Async XLA Ops:
  5.1 11.0 %collective-permute-start = (bf16[512,256]{1,0:T(8,128)(2,1)S(1)}, bf16[512,256]{1,0:T(8,128)(2,1)S(1)}, u32[]{:S(2)}, u32[]{:S(2)}) collective-permute-start(bf16[512,256]{1,0:T(8,128)(2,1)S(1)} %get-tuple-element.122), channel_id=1, source_target_pairs={{0,1},{1,2},{2,3},{3,4},{4,5},{5,6},{6,7},{7,8},{8,9},{9,10},{10,1... | collective-permute-start | bytes 786440 | tf_op jit(solution)/shard_map/while/body/eval_jaxpr/ppermute | solution.py:11
  5.6 10.5 %collective-permute-start.1 = (bf16[512,128]{1,0:T(8,128)(2,1)S(1)}, bf16[512,128]{1,0:T(8,128)(2,1)S(1)}, u32[]{:S(2)}, u32[]{:S(2)}) collective-permute-start(bf16[512,128]{1,0:T(8,128)(2,1)S(1)} %get-tuple-element.123), channel_id=1, source_target_pairs={{0,1},{1,2},{2,3},{3,4},{4,5},{5,6},{6,7},{7,8},{8,9},{9,10},{10,1... | collective-permute-start | bytes 393224 | tf_op jit(solution)/shard_map/while/body/eval_jaxpr/ppermute | solution.py:11
  17.9 10.0 %collective-permute-start = (bf16[512,256]{1,0:T(8,128)(2,1)S(1)}, bf16[512,256]{1,0:T(8,128)(2,1)S(1)}, u32[]{:S(2)}, u32[]{:S(2)}) collective-permute-start(bf16[512,256]{1,0:T(8,128)(2,1)S(1)} %get-tuple-element.122), channel_id=1, source_target_pairs={{0,1},{1,2},{2,3},{3,4},{4,5},{5,6},{6,7},{7,8},{8,9},{9,10},{10,1... | collective-permute-start | bytes 786440 | tf_op jit(solution)/shard_map/while/body/eval_jaxpr/ppermute | solution.py:11
  18.0 9.9 %collective-permute-start.1 = (bf16[512,128]{1,0:T(8,128)(2,1)S(1)}, bf16[512,128]{1,0:T(8,128)(2,1)S(1)}, u32[]{:S(2)}, u32[]{:S(2)}) collective-permute-start(bf16[512,128]{1,0:T(8,128)(2,1)S(1)} %get-tuple-element.123), channel_id=1, source_target_pairs={{0,1},{1,2},{2,3},{3,4},{4,5},{5,6},{6,7},{7,8},{8,9},{9,10},{10,1... | collective-permute-start | bytes 393224 | tf_op jit(solution)/shard_map/while/body/eval_jaxpr/ppermute | solution.py:11
  29.7 10.0 %collective-permute-start = (bf16[512,256]{1,0:T(8,128)(2,1)S(1)}, bf16[512,256]{1,0:T(8,128)(2,1)S(1)}, u32[]{:S(2)}, u32[]{:S(2)}) collective-permute-start(bf16[512,256]{1,0:T(8,128)(2,1)S(1)} %get-tuple-element.122), channel_id=1, source_target_pairs={{0,1},{1,2},{2,3},{3,4},{4,5},{5,6},{6,7},{7,8},{8,9},{9,10},{10,1... | collective-permute-start | bytes 786440 | tf_op jit(solution)/shard_map/while/body/eval_jaxpr/ppermute | solution.py:11
  29.8 9.9 %collective-permute-start.1 = (bf16[512,128]{1,0:T(8,128)(2,1)S(1)}, bf16[512,128]{1,0:T(8,128)(2,1)S(1)}, u32[]{:S(2)}, u32[]{:S(2)}) collective-permute-start(bf16[512,128]{1,0:T(8,128)(2,1)S(1)} %get-tuple-element.123), channel_id=1, source_target_pairs={{0,1},{1,2},{2,3},{3,4},{4,5},{5,6},{6,7},{7,8},{8,9},{9,10},{10,1... | collective-permute-start | bytes 393224 | tf_op jit(solution)/shard_map/while/body/eval_jaxpr/ppermute | solution.py:11
  41.5 10.0 %collective-permute-start = (bf16[512,256]{1,0:T(8,128)(2,1)S(1)}, bf16[512,256]{1,0:T(8,128)(2,1)S(1)}, u32[]{:S(2)}, u32[]{:S(2)}) collective-permute-start(bf16[512,256]{1,0:T(8,128)(2,1)S(1)} %get-tuple-element.122), channel_id=1, source_target_pairs={{0,1},{1,2},{2,3},{3,4},{4,5},{5,6},{6,7},{7,8},{8,9},{9,10},{10,1... | collective-permute-start | bytes 786440 | tf_op jit(solution)/shard_map/while/body/eval_jaxpr/ppermute | solution.py:11
  41.6 9.9 %collective-permute-start.1 = (bf16[512,128]{1,0:T(8,128)(2,1)S(1)}, bf16[512,128]{1,0:T(8,128)(2,1)S(1)}, u32[]{:S(2)}, u32[]{:S(2)}) collective-permute-start(bf16[512,128]{1,0:T(8,128)(2,1)S(1)} %get-tuple-element.123), channel_id=1, source_target_pairs={{0,1},{1,2},{2,3},{3,4},{4,5},{5,6},{6,7},{7,8},{8,9},{9,10},{10,1... | collective-permute-start | bytes 393224 | tf_op jit(solution)/shard_map/while/body/eval_jaxpr/ppermute | solution.py:11
  53.3 10.0 %collective-permute-start = (bf16[512,256]{1,0:T(8,128)(2,1)S(1)}, bf16[512,256]{1,0:T(8,128)(2,1)S(1)}, u32[]{:S(2)}, u32[]{:S(2)}) collective-permute-start(bf16[512,256]{1,0:T(8,128)(2,1)S(1)} %get-tuple-element.122), channel_id=1, source_target_pairs={{0,1},{1,2},{2,3},{3,4},{4,5},{5,6},{6,7},{7,8},{8,9},{9,10},{10,1... | collective-permute-start | bytes 786440 | tf_op jit(solution)/shard_map/while/body/eval_jaxpr/ppermute | solution.py:11
  53.4 9.9 %collective-permute-start.1 = (bf16[512,128]{1,0:T(8,128)(2,1)S(1)}, bf16[512,128]{1,0:T(8,128)(2,1)S(1)}, u32[]{:S(2)}, u32[]{:S(2)}) collective-permute-start(bf16[512,128]{1,0:T(8,128)(2,1)S(1)} %get-tuple-element.123), channel_id=1, source_target_pairs={{0,1},{1,2},{2,3},{3,4},{4,5},{5,6},{6,7},{7,8},{8,9},{9,10},{10,1... | collective-permute-start | bytes 393224 | tf_op jit(solution)/shard_map/while/body/eval_jaxpr/ppermute | solution.py:11
  65.1 10.0 %collective-permute-start = (bf16[512,256]{1,0:T(8,128)(2,1)S(1)}, bf16[512,256]{1,0:T(8,128)(2,1)S(1)}, u32[]{:S(2)}, u32[]{:S(2)}) collective-permute-start(bf16[512,256]{1,0:T(8,128)(2,1)S(1)} %get-tuple-element.122), channel_id=1, source_target_pairs={{0,1},{1,2},{2,3},{3,4},{4,5},{5,6},{6,7},{7,8},{8,9},{9,10},{10,1... | collective-permute-start | bytes 786440 | tf_op jit(solution)/shard_map/while/body/eval_jaxpr/ppermute | solution.py:11
  65.1 9.9 %collective-permute-start.1 = (bf16[512,128]{1,0:T(8,128)(2,1)S(1)}, bf16[512,128]{1,0:T(8,128)(2,1)S(1)}, u32[]{:S(2)}, u32[]{:S(2)}) collective-permute-start(bf16[512,128]{1,0:T(8,128)(2,1)S(1)} %get-tuple-element.123), channel_id=1, source_target_pairs={{0,1},{1,2},{2,3},{3,4},{4,5},{5,6},{6,7},{7,8},{8,9},{9,10},{10,1... | collective-permute-start | bytes 393224 | tf_op jit(solution)/shard_map/while/body/eval_jaxpr/ppermute | solution.py:11
  76.9 10.0 %collective-permute-start = (bf16[512,256]{1,0:T(8,128)(2,1)S(1)}, bf16[512,256]{1,0:T(8,128)(2,1)S(1)}, u32[]{:S(2)}, u32[]{:S(2)}) collective-permute-start(bf16[512,256]{1,0:T(8,128)(2,1)S(1)} %get-tuple-element.122), channel_id=1, source_target_pairs={{0,1},{1,2},{2,3},{3,4},{4,5},{5,6},{6,7},{7,8},{8,9},{9,10},{10,1... | collective-permute-start | bytes 786440 | tf_op jit(solution)/shard_map/while/body/eval_jaxpr/ppermute | solution.py:11
  76.9 9.9 %collective-permute-start.1 = (bf16[512,128]{1,0:T(8,128)(2,1)S(1)}, bf16[512,128]{1,0:T(8,128)(2,1)S(1)}, u32[]{:S(2)}, u32[]{:S(2)}) collective-permute-start(bf16[512,128]{1,0:T(8,128)(2,1)S(1)} %get-tuple-element.123), channel_id=1, source_target_pairs={{0,1},{1,2},{2,3},{3,4},{4,5},{5,6},{6,7},{7,8},{8,9},{9,10},{10,1... | collective-permute-start | bytes 393224 | tf_op jit(solution)/shard_map/while/body/eval_jaxpr/ppermute | solution.py:11
  88.6 10.0 %collective-permute-start = (bf16[512,256]{1,0:T(8,128)(2,1)S(1)}, bf16[512,256]{1,0:T(8,128)(2,1)S(1)}, u32[]{:S(2)}, u32[]{:S(2)}) collective-permute-start(bf16[512,256]{1,0:T(8,128)(2,1)S(1)} %get-tuple-element.122), channel_id=1, source_target_pairs={{0,1},{1,2},{2,3},{3,4},{4,5},{5,6},{6,7},{7,8},{8,9},{9,10},{10,1... | collective-permute-start | bytes 786440 | tf_op jit(solution)/shard_map/while/body/eval_jaxpr/ppermute | solution.py:11
  88.7 9.9 %collective-permute-start.1 = (bf16[512,128]{1,0:T(8,128)(2,1)S(1)}, bf16[512,128]{1,0:T(8,128)(2,1)S(1)}, u32[]{:S(2)}, u32[]{:S(2)}) collective-permute-start(bf16[512,128]{1,0:T(8,128)(2,1)S(1)} %get-tuple-element.123), channel_id=1, source_target_pairs={{0,1},{1,2},{2,3},{3,4},{4,5},{5,6},{6,7},{7,8},{8,9},{9,10},{10,1... | collective-permute-start | bytes 393224 | tf_op jit(solution)/shard_map/while/body/eval_jaxpr/ppermute | solution.py:11
  100.4 10.0 %collective-permute-start = (bf16[512,256]{1,0:T(8,128)(2,1)S(1)}, bf16[512,256]{1,0:T(8,128)(2,1)S(1)}, u32[]{:S(2)}, u32[]{:S(2)}) collective-permute-start(bf16[512,256]{1,0:T(8,128)(2,1)S(1)} %get-tuple-element.122), channel_id=1, source_target_pairs={{0,1},{1,2},{2,3},{3,4},{4,5},{5,6},{6,7},{7,8},{8,9},{9,10},{10,1... | collective-permute-start | bytes 786440 | tf_op jit(solution)/shard_map/while/body/eval_jaxpr/ppermute | solution.py:11
  100.5 9.9 %collective-permute-start.1 = (bf16[512,128]{1,0:T(8,128)(2,1)S(1)}, bf16[512,128]{1,0:T(8,128)(2,1)S(1)}, u32[]{:S(2)}, u32[]{:S(2)}) collective-permute-start(bf16[512,128]{1,0:T(8,128)(2,1)S(1)} %get-tuple-element.123), channel_id=1, source_target_pairs={{0,1},{1,2},{2,3},{3,4},{4,5},{5,6},{6,7},{7,8},{8,9},{9,10},{10,1... | collective-permute-start | bytes 393224 | tf_op jit(solution)/shard_map/while/body/eval_jaxpr/ppermute | solution.py:11
  112.2 10.0 %collective-permute-start = (bf16[512,256]{1,0:T(8,128)(2,1)S(1)}, bf16[512,256]{1,0:T(8,128)(2,1)S(1)}, u32[]{:S(2)}, u32[]{:S(2)}) collective-permute-start(bf16[512,256]{1,0:T(8,128)(2,1)S(1)} %get-tuple-element.122), channel_id=1, source_target_pairs={{0,1},{1,2},{2,3},{3,4},{4,5},{5,6},{6,7},{7,8},{8,9},{9,10},{10,1... | collective-permute-start | bytes 786440 | tf_op jit(solution)/shard_map/while/body/eval_jaxpr/ppermute | solution.py:11
  124.0 10.0 %collective-permute-start = (bf16[512,256]{1,0:T(8,128)(2,1)S(1)}, bf16[512,256]{1,0:T(8,128)(2,1)S(1)}, u32[]{:S(2)}, u32[]{:S(2)}) collective-permute-start(bf16[512,256]{1,0:T(8,128)(2,1)S(1)} %get-tuple-element.122), channel_id=1, source_target_pairs={{0,1},{1,2},{2,3},{3,4},{4,5},{5,6},{6,7},{7,8},{8,9},{9,10},{10,1... | collective-permute-start | bytes 786440 | tf_op jit(solution)/shard_map/while/body/eval_jaxpr/ppermute | solution.py:11
  135.8 10.0 %collective-permute-start = (bf16[512,256]{1,0:T(8,128)(2,1)S(1)}, bf16[512,256]{1,0:T(8,128)(2,1)S(1)}, u32[]{:S(2)}, u32[]{:S(2)}) collective-permute-start(bf16[512,256]{1,0:T(8,128)(2,1)S(1)} %get-tuple-element.122), channel_id=1, source_target_pairs={{0,1},{1,2},{2,3},{3,4},{4,5},{5,6},{6,7},{7,8},{8,9},{9,10},{10,1... | collective-permute-start | bytes 786440 | tf_op jit(solution)/shard_map/while/body/eval_jaxpr/ppermute | solution.py:11
  147.6 10.0 %collective-permute-start = (bf16[512,256]{1,0:T(8,128)(2,1)S(1)}, bf16[512,256]{1,0:T(8,128)(2,1)S(1)}, u32[]{:S(2)}, u32[]{:S(2)}) collective-permute-start(bf16[512,256]{1,0:T(8,128)(2,1)S(1)} %get-tuple-element.122), channel_id=1, source_target_pairs={{0,1},{1,2},{2,3},{3,4},{4,5},{5,6},{6,7},{7,8},{8,9},{9,10},{10,1... | collective-permute-start | bytes 786440 | tf_op jit(solution)/shard_map/while/body/eval_jaxpr/ppermute | solution.py:11
  159.4 10.0 %collective-permute-start = (bf16[512,256]{1,0:T(8,128)(2,1)S(1)}, bf16[512,256]{1,0:T(8,128)(2,1)S(1)}, u32[]{:S(2)}, u32[]{:S(2)}) collective-permute-start(bf16[512,256]{1,0:T(8,128)(2,1)S(1)} %get-tuple-element.122), channel_id=1, source_target_pairs={{0,1},{1,2},{2,3},{3,4},{4,5},{5,6},{6,7},{7,8},{8,9},{9,10},{10,1... | collective-permute-start | bytes 786440 | tf_op jit(solution)/shard_map/while/body/eval_jaxpr/ppermute | solution.py:11
  171.1 10.0 %collective-permute-start = (bf16[512,256]{1,0:T(8,128)(2,1)S(1)}, bf16[512,256]{1,0:T(8,128)(2,1)S(1)}, u32[]{:S(2)}, u32[]{:S(2)}) collective-permute-start(bf16[512,256]{1,0:T(8,128)(2,1)S(1)} %get-tuple-element.122), channel_id=1, source_target_pairs={{0,1},{1,2},{2,3},{3,4},{4,5},{5,6},{6,7},{7,8},{8,9},{9,10},{10,1... | collective-permute-start | bytes 786440 | tf_op jit(solution)/shard_map/while/body/eval_jaxpr/ppermute | solution.py:11
  (9 other events, 62.3 us)
where the time goes:
time: 185 us; the launch traced here: 184 us
  waiting for transfers between devices  143 us (77%)
  matrix products  25.2 us (14%)
  other arithmetic  7.28 us (4%)
  starting transfers between devices  4.76 us (3%)
  local copies, waits for them, and re-layouts  2.18 us (1%)
    ppermute x30, waiting for transfers between devices, from_behind(): lax.ppermute(array, axis, [(i, (i + by) % peers) for i in range(peers)])  143 us
    dot_general x16, matrix products, pair_terms(): near_vu = jnp.dot(kernel_bf, far_right, preferred_element_type=jnp.float32)  7.88 us
    dot_general x16, matrix products, pair_terms(): lax.dot_general(own_left, far_right, (((1,), (1,)), ((), ())), preferred_...  6.04 us
    dot_general x16, matrix products, pair_terms(): jnp.dot(mixed_bf, far_x, preferred_element_type=jnp.float32)  5.96 us
    dot_general x16, matrix products, pair_terms(): lax.dot_general(own_x, far_x, (((1,), (1,)), ((), ())), preferred_element...  5.36 us
    ppermute x30, starting transfers between devices, from_behind(): lax.ppermute(array, axis, [(i, (i + by) % peers) for i in range(peers)])  4.76 us
  transfers between devices with their start and end apart: 30, of which 15 were waited for; matrix products, arithmetic and copies ran while one was open for 1% of the time, Pallas kernels for 0%

commit v1 on v0

v1 whole, which is shorter than its diff:
```python
import functools
import math

import jax
import jax.numpy as jnp
from jax import lax
from jax.experimental import pallas as pl
from jax.experimental.pallas import tpu as pltpu
from jax.sharding import PartitionSpec as P

MESH = pl.DeviceIdType.MESH
CHUNKS = 2
PARTS = 2
NT = (((1,), (1,)), ((), ()))


def row_squares(block):
    wide = block.astype(jnp.float32)
    return jnp.sum(wide * wide, axis=1, keepdims=True)


def column_squares(block):
    wide = block.astype(jnp.float32)
    square = wide * wide
    high = square.astype(jnp.bfloat16)
    low = (square - high.astype(jnp.float32)).astype(jnp.bfloat16)
    ones = jnp.ones((16, block.shape[1]), jnp.bfloat16)
    total = lax.dot_general(ones, high, NT, preferred_element_type=jnp.float32)
    total += lax.dot_general(ones, low, NT, preferred_element_type=jnp.float32)
    return total[:1]


def pair_block(rows_x, rows_left, rows_sq, cols_x, cols_right, cols_sq):
    slope = 2.0 * math.log2(math.e) / rows_x.shape[1]
    gram = lax.dot_general(rows_x, cols_x, NT, preferred_element_type=jnp.float32)
    inner = lax.dot_general(rows_left, cols_right, NT, preferred_element_type=jnp.float32)
    kernel = jnp.exp2(gram * slope - rows_sq - cols_sq)
    mixed = kernel * inner
    vu = jnp.dot(kernel.astype(jnp.bfloat16), cols_right, preferred_element_type=jnp.float32)
    grad = jnp.dot(mixed.astype(jnp.bfloat16), cols_x, preferred_element_type=jnp.float32)
    sums = mixed[:, :128]
    for at in range(128, mixed.shape[1], 128):
        sums += mixed[:, at : at + 128]
    return vu, grad, sums


def swap_halves(right):
    half = right.shape[1] // 2
    return jnp.concatenate([right[:, half:], right[:, :half]], axis=1)


def paired_kernel(
    depth, points, left, right, out_vu, out_grad,
    blocks, lefts, squares, acc_vu, acc_grad, acc_sum, res_out, res_in,
    recv, send_part, send_mid, send_sib, send_side, send_res, recv_res,
):
    rows, feat = points.shape
    vecs = left.shape[1]
    size = rows // CHUNKS
    group, me = lax.axis_index("groups"), lax.axis_index("blk")
    z, y, c = me // 4, lax.rem(me // 2, 2), lax.rem(me, 2)
    upper = z // 2
    inner = jnp.logical_or(z == 1, z == 2)
    part_z = z + 1 - 2 * lax.rem(z, 2)

    def slot_of(plane, yy, cc):
        return plane * 4 + yy * 2 + cc

    partner = slot_of(part_z, y, c)
    mid = slot_of(3 - z, y, c)
    sib = slot_of(z, y, 1 - c)
    side = slot_of(z, 1 - y, c)
    first = jnp.where(inner, 3 - z, z)
    second = jnp.where(inner, 3 * (1 - upper), part_z)

    def view(slot, chunk):
        return blocks.at[slot, pl.ds(pl.multiple_of(chunk * size, size), size), :]

    def copy(slot, chunk, send, target):
        return pltpu.make_async_remote_copy(
            src_ref=view(slot, chunk),
            dst_ref=view(slot, chunk),
            send_sem=send,
            recv_sem=recv.at[slot * CHUNKS + chunk],
            device_id=(group, target),
            device_id_type=MESH,
        )

    def plane_of(t):
        return jnp.where(t < CHUNKS, first, second)

    def arrived(slot, chunk):
        copy(slot, chunk, send_part.at[0], partner).wait_recv()

    barrier = pltpu.get_barrier_semaphore()
    for other in (partner, sib, side):
        pl.semaphore_signal(barrier, inc=1, device_id=(group, other), device_id_type=MESH)

    @pl.when(inner)
    def _():
        pl.semaphore_signal(barrier, inc=1, device_id=(group, mid), device_id_type=MESH)

    blocks[me, :, :feat] = points[...]
    blocks[me, :, feat:] = jnp.concatenate([right[...], left[...]], axis=1)
    pl.semaphore_wait(barrier, jnp.where(inner, 4, 3))

    for chunk in range(CHUNKS):
        copy(me, chunk, send_part.at[chunk], partner).start()

        @pl.when(inner)
        def _():
            copy(me, chunk, send_mid.at[chunk], mid).start()

    half_log = math.log2(math.e) / feat

    def set_rows(which, slot):
        block = blocks[slot]
        lefts[which] = swap_halves(block[:, feat:])
        squares[which] = jnp.broadcast_to(row_squares(block[:, :feat]) * half_log, (rows, 128))

    set_rows(0, me)
    acc_vu[...] = jnp.zeros_like(acc_vu)
    acc_grad[...] = jnp.zeros_like(acc_grad)
    acc_sum[...] = jnp.zeros_like(acc_sum)

    strip = 256 if rows % 256 == 0 else rows

    def unit(which, row_slot, slot, chunk):
        span = pl.ds(pl.multiple_of(chunk * size, size), size)
        cols_x = blocks[slot, span, :feat]
        cols_right = blocks[slot, span, feat:]
        cols_sq = column_squares(cols_x) * half_log
        for at in range(0, rows, strip):
            here = pl.ds(at, strip)
            sq = squares[which, here, :]
            vu, grad, sums = pair_block(
                blocks[row_slot, here, :feat], lefts[which, here, :],
                jnp.concatenate([sq] * (size // 128), axis=1),
                cols_x, cols_right, cols_sq,
            )
            acc_vu[which, here, :] += vu
            acc_grad[which, here, :] += grad
            acc_sum[which, here, :] += sums

    def result(piece):
        span = rows // PARTS
        at = pl.ds(piece * span, span)
        return pltpu.make_async_remote_copy(
            src_ref=res_out.at[at, :],
            dst_ref=res_in.at[at, :],
            send_sem=send_res.at[piece],
            recv_sem=recv_res.at[piece],
            device_id=(group, partner),
            device_id_type=MESH,
        )

    def step(s, carry):
        fresh = s < 2 * CHUNKS

        @pl.when(fresh)
        def _():
            chunk = lax.rem(s, CHUNKS)
            slot = slot_of(plane_of(s), y, c)

            @pl.when(inner)
            def _():
                arrived(slot, chunk)

            @pl.when(jnp.logical_and(jnp.logical_not(inner), s == CHUNKS))
            def _():
                for piece in range(CHUNKS):
                    arrived(partner, piece)

            copy(slot, chunk, send_side.at[s], side).start()
            copy(slot, chunk, send_sib.at[s], sib).start()

            @pl.when(jnp.logical_and(inner, s < CHUNKS))
            def _():
                arrived(partner, chunk)
                copy(partner, chunk, send_mid.at[CHUNKS + chunk], mid).start()

        @pl.when(s >= 1)
        def _():
            t = s - 1
            chunk = lax.rem(t, CHUNKS)
            slot = slot_of(plane_of(t), 1 - y, c)
            arrived(slot, chunk)
            copy(slot, chunk, send_sib.at[2 * CHUNKS + t], sib).start()
            arrived(slot_of(plane_of(t), 1 - y, 1 - c), chunk)

        @pl.when(fresh)
        def _():
            arrived(slot_of(plane_of(s), y, 1 - c), lax.rem(s, CHUNKS))

        @pl.when(s == CHUNKS)
        def _():
            set_rows(1, partner)

        def job(j, carry):
            kind = j // 2
            back = jnp.logical_or(jnp.logical_or(kind == 1, kind == 3), kind == 5)
            catch = kind < 2
            t = jnp.where(catch, s - CHUNKS, jnp.where(back, s - 1, s))
            low = jnp.where(jnp.logical_or(kind == 2, kind == 3), CHUNKS, 0)
            ok = jnp.logical_and(t >= low, t < 2 * CHUNKS)
            ok = jnp.logical_and(ok, jnp.logical_or(jnp.logical_not(catch), fresh))
            which = jnp.where(kind < 4, 1, 0)

            @pl.when(ok)
            def _():
                yy = jnp.where(back, 1 - y, y)
                cc = jnp.where(lax.rem(j, 2) == 0, c, 1 - c)
                slot = slot_of(plane_of(t), yy, cc)
                unit(which, jnp.where(which == 0, me, partner), slot, lax.rem(t, CHUNKS))

            @pl.when(jnp.logical_and(j == 7, jnp.logical_not(fresh)))
            def _():
                for piece in range(PARTS):
                    span = rows // PARTS
                    at = pl.ds(piece * span, span)
                    total = jnp.sum(acc_sum[1, at, :], axis=1, keepdims=True)
                    x = blocks[partner, at, :feat].astype(jnp.float32)
                    res_out[at, feat:] = acc_vu[1, at, :].astype(jnp.bfloat16)
                    res_out[at, :feat] = (acc_grad[1, at, :] - total * x).astype(jnp.bfloat16)
                    result(piece).start()

            return carry

        return lax.fori_loop(0, 12, job, carry)

    lax.fori_loop(0, 2 * CHUNKS + 1, step, 0)

    scale = 1.0 / math.sqrt(rows * depth)
    for piece in range(PARTS):
        span = rows // PARTS
        at = pl.ds(piece * span, span)
        total = jnp.sum(acc_sum[0, at, :], axis=1, keepdims=True)
        x = blocks[me, at, :feat].astype(jnp.float32)
        grad = acc_grad[0, at, :] - total * x
        result(piece).wait_recv()
        out_vu[at, :] = (acc_vu[0, at, :] + res_in[at, feat:].astype(jnp.float32)) * scale
        out_grad[at, :] = (grad + res_in[at, :feat].astype(jnp.float32)) * scale

    for piece in range(PARTS):
        result(piece).wait_send()
    for chunk in range(CHUNKS):
        copy(me, chunk, send_part.at[chunk], partner).wait_send()
    for t in range(2 * CHUNKS):
        chunk = t % CHUNKS
        plane = first if t < CHUNKS else second
        copy(slot_of(plane, y, c), chunk, send_side.at[t], side).wait_send()
        copy(slot_of(plane, y, c), chunk, send_sib.at[t], sib).wait_send()
        copy(slot_of(plane, 1 - y, c), chunk, send_sib.at[2 * CHUNKS + t], sib).wait_send()

    @pl.when(inner)
    def _():
        for chunk in range(CHUNKS):
            copy(me, chunk, send_mid.at[chunk], mid).wait_send()
            copy(partner, chunk, send_mid.at[CHUNKS + chunk], mid).wait_send()


def paired_device(depth, points, left, right):
    rows, feat = points.shape
    wide = 2 * left.shape[1]
    bf, f32, dma = jnp.bfloat16, jnp.float32, pltpu.SemaphoreType.DMA
    return tuple(
        pl.pallas_call(
            functools.partial(paired_kernel, depth),
            out_shape=(
                jax.ShapeDtypeStruct((rows, wide), f32),
                jax.ShapeDtypeStruct((rows, feat), f32),
            ),
            in_specs=[pl.BlockSpec(memory_space=pltpu.VMEM)] * 3,
            out_specs=[pl.BlockSpec(memory_space=pltpu.VMEM)] * 2,
            scratch_shapes=[
                pltpu.VMEM((depth, rows, feat + wide), bf),
                pltpu.VMEM((2, rows, wide), bf),
                pltpu.VMEM((2, rows, 128), f32),
                pltpu.VMEM((2, rows, wide), f32),
                pltpu.VMEM((2, rows, feat), f32),
                pltpu.VMEM((2, rows, 128), f32),
                pltpu.VMEM((rows, feat + wide), bf),
                pltpu.VMEM((rows, feat + wide), bf),
                dma((depth * CHUNKS,)),
                dma((CHUNKS,)),
                dma((2 * CHUNKS,)),
                dma((4 * CHUNKS,)),
                dma((2 * CHUNKS,)),
                dma((PARTS,)),
                dma((PARTS,)),
            ],
            compiler_params=pltpu.CompilerParams(
                collective_id=0, has_side_effects=True, vmem_limit_bytes=48 * 2**20
            ),
        )(points, left, right)
    )


def gathered_kernel(depth, points, left, right, all_x, all_right, out_vu, out_grad, acc_sum):
    step = pl.program_id(0)
    feat = points.shape[1]
    half_log = math.log2(math.e) / feat
    scale = 1.0 / math.sqrt(points.shape[0] * depth)

    @pl.when(step == 0)
    def _():
        out_vu[...] = jnp.zeros_like(out_vu)
        out_grad[...] = jnp.zeros_like(out_grad)
        acc_sum[...] = jnp.zeros_like(acc_sum)

    own_left = jnp.concatenate([left[...], right[...]], axis=1)
    vu, grad, sums = pair_block(
        points[...], own_left, row_squares(points[...]) * half_log,
        all_x[...], all_right[...], column_squares(all_x[...]) * half_log,
    )
    out_vu[...] += vu
    out_grad[...] += grad
    acc_sum[...] += sums

    @pl.when(step == pl.num_programs(0) - 1)
    def _():
        total = jnp.sum(acc_sum[...], axis=1, keepdims=True)
        out_vu[...] = out_vu[...] * scale
        out_grad[...] = (out_grad[...] - total * points[...].astype(jnp.float32)) * scale


def gathered_device(depth, points, left, right):
    rows, feat = points.shape
    wide = 2 * left.shape[1]
    own_right = jnp.concatenate([right, left], axis=1)
    all_x = lax.all_gather(points, "blk", tiled=True)
    all_right = lax.all_gather(own_right, "blk", tiled=True)
    tile = 256

    def whole(array):
        return pl.BlockSpec(array.shape, lambda i: (0, 0))

    return tuple(
        pl.pallas_call(
            functools.partial(gathered_kernel, depth),
            grid=(rows * depth // tile,),
            out_shape=(
                jax.ShapeDtypeStruct((rows, wide), jnp.float32),
                jax.ShapeDtypeStruct((rows, feat), jnp.float32),
            ),
            in_specs=[
                whole(points), whole(left), whole(right),
                pl.BlockSpec((tile, feat), lambda i: (i, 0)),
                pl.BlockSpec((tile, wide), lambda i: (i, 0)),
            ],
            out_specs=[
                pl.BlockSpec((rows, wide), lambda i: (0, 0)),
                pl.BlockSpec((rows, feat), lambda i: (0, 0)),
            ],
            scratch_shapes=[pltpu.VMEM((rows, 128), jnp.float32)],
            compiler_params=pltpu.CompilerParams(vmem_limit_bytes=32 * 2**20),
        )(points, left, right, all_x, all_right)
    )


def solution(mesh):
    depth = mesh.shape["blk"]
    per_device = paired_device if depth == 16 else gathered_device
    spec = P(("groups", "blk"), None)
    return jax.shard_map(
        functools.partial(per_device, depth),
        mesh=mesh,
        in_specs=(spec, spec, spec),
        out_specs=(spec, spec),
        check_vma=False,
    )
```

time: 185 us -> 58.4 us (0.32)
  waiting for transfers between devices: 143 us -> 0 us
  Pallas kernels: 0 us -> 54.9 us
  matrix products: 25.2 us -> 0 us
  other arithmetic: 7.28 us -> 0 us
  starting transfers between devices: 4.76 us -> 0 us
    ppermute x30 -> x0, waiting for transfers between devices: 143 us -> none  [from_behind(): lax.ppermute(array, axis, [(i, (i + by) % peers) for i in range(peers)])]
    pallas_call x0 -> x1, Pallas kernels: none -> 54.9 us  [paired_device(): pl.pallas_call(functools.partial(paired_kernel, depth), out_shape=(jax.Sh...]
    dot_general x64 -> x0, matrix products: 25.2 us -> none  [the longest x16 7.88 us: pair_terms(): near_vu = jnp.dot(kernel_bf, far_right, preferred_element_type=jnp.float32)]
    reduce_sum x31 -> x0, other arithmetic: 5.56 us -> none  [the longest x16 3.35 us: pair_terms(): own_sq = jnp.sum(jnp.square(own_x.astype(jnp.float32)), axis=1)]
    ppermute x30 -> x0, starting transfers between devices: 4.76 us -> none  [from_behind(): lax.ppermute(array, axis, [(i, (i + by) % peers) for i in range(peers)])]
  transfers between devices with their start and end apart: 30 -> 0, of which waited for: 15 -> 0; matrix products, arithmetic and copies ran while one was open for 1% -> 0% of each run, Pallas kernels for 0% -> 0%
where the time goes in v1:
time: 58.4 us; the launch traced here: 58.2 us
  Pallas kernels  54.9 us (94%)
  local copies, waits for them, and re-layouts  2.62 us (4%)
  between operations  0.68 us (1%)
    pallas_call x1, Pallas kernels, paired_device(): pl.pallas_call(functools.partial(paired_kernel, depth), out_shape=(jax.Sh...  54.9 us
    unnamed x8, local copies, waits for them, and re-layouts  2.62 us

profile of v1, /device:TPU:0, one launch (start us, length us, event | category | flops | bytes accessed | tf_op | source)
XLA Modules:
  0.0 58.2 jit_solution(17013153230810875612)
XLA Ops:
  0.6 0.0 copy-start.1
  0.6 0.0 copy-start
  0.6 1.0 %copy.5.left = bf16[512,64]{1,0:T(8,128)(2,1)S(1)} copy(bf16[512,64]{0,1:T(8,128)(2,1)} %param.4) | data formatting | bytes 131072 | tf_op args[1]
  1.7 0.0 copy-done.1
  1.7 0.1 copy.6.right
  1.8 0.0 copy-done
  1.8 54.9 %shard_map.50 = (f32[512,128]{1,0:T(8,128)S(1)}, f32[512,256]{1,0:T(8,128)S(1)}) custom-call(bf16[512,256]{1,0:T(8,128)(2,1)S(1)} %copy-done, bf16[512,64]{1,0:T(8,128)(2,1)S(1)} %copy.5.left, bf16[512,64]{1,0:T(8,128)(2,1)S(1)} %copy.6.right), custom_call_target="tpu_custom_call" | custom-call | tf_op jit(solution)/shard_map/pallas_call | solution.py:267
  56.7 0.7 %copy.9 = f32[512,128]{1,0:T(8,128)} copy(f32[512,128]{1,0:T(8,128)S(1)} %get-tuple-element.4) | data formatting | bytes 524288
  57.4 0.8 %copy.10 = f32[512,256]{1,0:T(8,128)} copy(f32[512,256]{1,0:T(8,128)S(1)} %get-tuple-element.5) | data formatting | bytes 1048576
Async XLA Ops:
  0.6 1.0 %copy-start.1 = (bf16[512,64]{0,1:T(8,128)(2,1)S(1)}, bf16[512,64]{0,1:T(8,128)(2,1)}, u32[]{:S(2)}) copy-start(bf16[512,64]{0,1:T(8,128)(2,1)} %param.5) | copy-start | bytes 196612
  0.6 1.2 %copy-start = (bf16[512,256]{1,0:T(8,128)(2,1)S(1)}, bf16[512,256]{1,0:T(8,128)(2,1)}, u32[]{:S(2)}) copy-start(bf16[512,256]{1,0:T(8,128)(2,1)} %points.1) | copy-start | bytes 786436

commit v2 on v1

--- a/solution.py
+++ b/solution.py
@@ -9,8 +9,8 @@
 from jax.sharding import PartitionSpec as P
 
 MESH = pl.DeviceIdType.MESH
-CHUNKS = 2
-PARTS = 2
+CHUNKS = 4
+PARTS = 4
 NT = (((1,), (1,)), ((), ()))
 
 
@@ -86,9 +86,6 @@
             device_id_type=MESH,
         )
 
-    def plane_of(t):
-        return jnp.where(t < CHUNKS, first, second)
-
     def arrived(slot, chunk):
         copy(slot, chunk, send_part.at[0], partner).wait_recv()
 
@@ -123,19 +120,21 @@
     acc_grad[...] = jnp.zeros_like(acc_grad)
     acc_sum[...] = jnp.zeros_like(acc_sum)
 
-    strip = 256 if rows % 256 == 0 else rows
-
-    def unit(which, row_slot, slot, chunk):
-        span = pl.ds(pl.multiple_of(chunk * size, size), size)
-        cols_x = blocks[slot, span, :feat]
-        cols_right = blocks[slot, span, feat:]
+    strip = rows
+
+    def unit(which, order, yy, begin, length):
+        first_slot = slot_of(first if order == 0 else second, yy, 0)
+        span = pl.ds(begin, length)
+        cols_x = blocks[pl.ds(first_slot, 2), span, :feat].reshape(2 * length, feat)
+        cols_right = blocks[pl.ds(first_slot, 2), span, feat:].reshape(2 * length, -1)
         cols_sq = column_squares(cols_x) * half_log
+        row_slot = partner if which else me
         for at in range(0, rows, strip):
             here = pl.ds(at, strip)
             sq = squares[which, here, :]
             vu, grad, sums = pair_block(
                 blocks[row_slot, here, :feat], lefts[which, here, :],
-                jnp.concatenate([sq] * (size // 128), axis=1),
+                jnp.concatenate([sq] * (2 * length // 128), axis=1),
                 cols_x, cols_right, cols_sq,
             )
             acc_vu[which, here, :] += vu
@@ -154,81 +153,89 @@
             device_id_type=MESH,
         )
 
-    def step(s, carry):
-        fresh = s < 2 * CHUNKS
-
-        @pl.when(fresh)
+    def planes(t):
+        return first if t < CHUNKS else second
+
+    def from_line(t):
+        chunk = t % CHUNKS
+        slot = slot_of(planes(t), y, c)
+
+        @pl.when(inner)
         def _():
-            chunk = lax.rem(s, CHUNKS)
-            slot = slot_of(plane_of(s), y, c)
+            arrived(slot, chunk)
+
+        copy(slot, chunk, send_side.at[t], side).start()
+        copy(slot, chunk, send_sib.at[t], sib).start()
+        if t < CHUNKS:
+            arrived(partner, chunk)
 
             @pl.when(inner)
             def _():
-                arrived(slot, chunk)
-
-            @pl.when(jnp.logical_and(jnp.logical_not(inner), s == CHUNKS))
-            def _():
-                for piece in range(CHUNKS):
-                    arrived(partner, piece)
-
-            copy(slot, chunk, send_side.at[s], side).start()
-            copy(slot, chunk, send_sib.at[s], sib).start()
-
-            @pl.when(jnp.logical_and(inner, s < CHUNKS))
-            def _():
-                arrived(partner, chunk)
                 copy(partner, chunk, send_mid.at[CHUNKS + chunk], mid).start()
 
-        @pl.when(s >= 1)
-        def _():
-            t = s - 1
-            chunk = lax.rem(t, CHUNKS)
-            slot = slot_of(plane_of(t), 1 - y, c)
-            arrived(slot, chunk)
-            copy(slot, chunk, send_sib.at[2 * CHUNKS + t], sib).start()
-            arrived(slot_of(plane_of(t), 1 - y, 1 - c), chunk)
-
-        @pl.when(fresh)
-        def _():
-            arrived(slot_of(plane_of(s), y, 1 - c), lax.rem(s, CHUNKS))
-
-        @pl.when(s == CHUNKS)
-        def _():
+    def from_side(t):
+        chunk = t % CHUNKS
+        slot = slot_of(planes(t), 1 - y, c)
+        arrived(slot, chunk)
+        copy(slot, chunk, send_sib.at[2 * CHUNKS + t], sib).start()
+
+    def sib_line(t):
+        arrived(slot_of(planes(t), y, 1 - c), t % CHUNKS)
+
+    def sib_side(t):
+        arrived(slot_of(planes(t), 1 - y, 1 - c), t % CHUNKS)
+
+    half = rows // 2
+    for t in range(2 * CHUNKS):
+        from_line(t)
+        if t >= 1:
+            from_side(t - 1)
+        if t == 2:
+            for u in (0, 1):
+                sib_line(u)
+            unit(0, 0, y, 0, half)
+        elif t == 3:
+            for u in (0, 1):
+                sib_side(u)
+            unit(0, 0, 1 - y, 0, half)
+        elif t == 4:
             set_rows(1, partner)
-
-        def job(j, carry):
-            kind = j // 2
-            back = jnp.logical_or(jnp.logical_or(kind == 1, kind == 3), kind == 5)
-            catch = kind < 2
-            t = jnp.where(catch, s - CHUNKS, jnp.where(back, s - 1, s))
-            low = jnp.where(jnp.logical_or(kind == 2, kind == 3), CHUNKS, 0)
-            ok = jnp.logical_and(t >= low, t < 2 * CHUNKS)
-            ok = jnp.logical_and(ok, jnp.logical_or(jnp.logical_not(catch), fresh))
-            which = jnp.where(kind < 4, 1, 0)
-
-            @pl.when(ok)
-            def _():
-                yy = jnp.where(back, 1 - y, y)
-                cc = jnp.where(lax.rem(j, 2) == 0, c, 1 - c)
-                slot = slot_of(plane_of(t), yy, cc)
-                unit(which, jnp.where(which == 0, me, partner), slot, lax.rem(t, CHUNKS))
-
-            @pl.when(jnp.logical_and(j == 7, jnp.logical_not(fresh)))
-            def _():
-                for piece in range(PARTS):
-                    span = rows // PARTS
-                    at = pl.ds(piece * span, span)
-                    total = jnp.sum(acc_sum[1, at, :], axis=1, keepdims=True)
-                    x = blocks[partner, at, :feat].astype(jnp.float32)
-                    res_out[at, feat:] = acc_vu[1, at, :].astype(jnp.bfloat16)
-                    res_out[at, :feat] = (acc_grad[1, at, :] - total * x).astype(jnp.bfloat16)
-                    result(piece).start()
-
-            return carry
-
-        return lax.fori_loop(0, 12, job, carry)
-
-    lax.fori_loop(0, 2 * CHUNKS + 1, step, 0)
+            for u in (2, 3):
+                sib_line(u)
+            unit(1, 0, y, 0, rows)
+        elif t == 5:
+            for u in (2, 3):
+                sib_side(u)
+            unit(1, 0, 1 - y, 0, rows)
+        elif t == 6:
+            for u in (4, 5):
+                sib_line(u)
+            unit(1, 1, y, 0, half)
+            unit(0, 0, y, half, half)
+        elif t == 7:
+            for u in (4, 5):
+                sib_side(u)
+            unit(1, 1, 1 - y, 0, half)
+            for u in (6, 7):
+                sib_line(u)
+            unit(1, 1, y, half, half)
+    from_side(2 * CHUNKS - 1)
+    for u in (6, 7):
+        sib_side(u)
+    unit(1, 1, 1 - y, half, half)
+
+    for piece in range(PARTS):
+        span = rows // PARTS
+        at = pl.ds(piece * span, span)
+        total = jnp.sum(acc_sum[1, at, :], axis=1, keepdims=True)
+        x = blocks[partner, at, :feat].astype(jnp.float32)
+        res_out[at, feat:] = acc_vu[1, at, :].astype(jnp.bfloat16)
+        res_out[at, :feat] = (acc_grad[1, at, :] - total * x).astype(jnp.bfloat16)
+        result(piece).start()
+
+    unit(0, 0, 1 - y, half, half)
+    unit(0, 1, y, 0, rows)
+    unit(0, 1, 1 - y, 0, rows)
 
     scale = 1.0 / math.sqrt(rows * depth)
     for piece in range(PARTS):

time: 58.4 us -> 47.3 us (0.81)
  Pallas kernels: 54.9 us -> 43.8 us
    pallas_call x1, Pallas kernels: 54.9 us -> 43.8 us  [paired_device(): pl.pallas_call(functools.partial(paired_kernel, depth), out_shape=(jax.Sh...]
where the time goes in v2:
time: 47.3 us; the launch traced here: 47.1 us
  Pallas kernels  43.8 us (93%)
  local copies, waits for them, and re-layouts  2.62 us (6%)
  between operations  0.68 us (1%)
    pallas_call x1, Pallas kernels, paired_device(): pl.pallas_call(functools.partial(paired_kernel, depth), out_shape=(jax.Sh...  43.8 us
    unnamed x8, local copies, waits for them, and re-layouts  2.62 us

profile of v2, /device:TPU:0, one launch (start us, length us, event | category | flops | bytes accessed | tf_op | source)
XLA Modules:
  0.0 47.1 jit_solution(11976454583856619250)
XLA Ops:
  0.6 0.0 copy-start.1
  0.6 0.0 copy-start
  0.6 1.0 %copy.5.left = bf16[512,64]{1,0:T(8,128)(2,1)S(1)} copy(bf16[512,64]{0,1:T(8,128)(2,1)} %param.4) | data formatting | bytes 131072 | tf_op args[1]
  1.7 0.0 copy-done.1
  1.7 0.1 copy.6.right
  1.8 0.0 copy-done
  1.8 43.8 %shard_map.50 = (f32[512,128]{1,0:T(8,128)S(1)}, f32[512,256]{1,0:T(8,128)S(1)}) custom-call(bf16[512,256]{1,0:T(8,128)(2,1)S(1)} %copy-done, bf16[512,64]{1,0:T(8,128)(2,1)S(1)} %copy.5.left, bf16[512,64]{1,0:T(8,128)(2,1)S(1)} %copy.6.right), custom_call_target="tpu_custom_call" | custom-call | tf_op jit(solution)/shard_map/pallas_call | solution.py:274
  45.6 0.7 %copy.9 = f32[512,128]{1,0:T(8,128)} copy(f32[512,128]{1,0:T(8,128)S(1)} %get-tuple-element.4) | data formatting | bytes 524288
  46.3 0.8 %copy.10 = f32[512,256]{1,0:T(8,128)} copy(f32[512,256]{1,0:T(8,128)S(1)} %get-tuple-element.5) | data formatting | bytes 1048576
Async XLA Ops:
  0.6 1.0 %copy-start.1 = (bf16[512,64]{0,1:T(8,128)(2,1)S(1)}, bf16[512,64]{0,1:T(8,128)(2,1)}, u32[]{:S(2)}) copy-start(bf16[512,64]{0,1:T(8,128)(2,1)} %param.5) | copy-start | bytes 196612
  0.6 1.2 %copy-start = (bf16[512,256]{1,0:T(8,128)(2,1)S(1)}, bf16[512,256]{1,0:T(8,128)(2,1)}, u32[]{:S(2)}) copy-start(bf16[512,256]{1,0:T(8,128)(2,1)} %points.1) | copy-start | bytes 786436

commit v3 on v2

--- a/solution.py
+++ b/solution.py
@@ -10,6 +10,8 @@
 
 MESH = pl.DeviceIdType.MESH
 CHUNKS = 4
+WINDOW = 3
+SKEW = 2
 PARTS = 4
 NT = (((1,), (1,)), ((), ()))
 
@@ -101,12 +103,15 @@
     blocks[me, :, feat:] = jnp.concatenate([right[...], left[...]], axis=1)
     pl.semaphore_wait(barrier, jnp.where(inner, 4, 3))
 
-    for chunk in range(CHUNKS):
+    def to_mid(t):
+        return copy(me if t < CHUNKS else partner, t % CHUNKS, send_mid.at[t], mid)
+
+    for chunk in range(WINDOW):
         copy(me, chunk, send_part.at[chunk], partner).start()
 
         @pl.when(inner)
         def _():
-            copy(me, chunk, send_mid.at[chunk], mid).start()
+            to_mid(chunk).start()
 
     half_log = math.log2(math.e) / feat
 
@@ -168,10 +173,13 @@
         copy(slot, chunk, send_sib.at[t], sib).start()
         if t < CHUNKS:
             arrived(partner, chunk)
+            if chunk + WINDOW < CHUNKS:
+                copy(me, chunk + WINDOW, send_part.at[chunk + WINDOW], partner).start()
+        if t + WINDOW < 2 * CHUNKS:
 
             @pl.when(inner)
             def _():
-                copy(partner, chunk, send_mid.at[CHUNKS + chunk], mid).start()
+                to_mid(t + WINDOW).start()
 
     def from_side(t):
         chunk = t % CHUNKS
@@ -186,42 +194,45 @@
         arrived(slot_of(planes(t), 1 - y, 1 - c), t % CHUNKS)
 
     half = rows // 2
+    quarter = CHUNKS // 2
+
+    def line_ready(piece):
+        for u in range(piece * quarter, (piece + 1) * quarter):
+            sib_line(u)
+
+    def side_ready(piece):
+        for u in range(piece * quarter, (piece + 1) * quarter):
+            sib_side(u)
+
     for t in range(2 * CHUNKS):
         from_line(t)
-        if t >= 1:
-            from_side(t - 1)
-        if t == 2:
-            for u in (0, 1):
-                sib_line(u)
+        if t >= SKEW:
+            from_side(t - SKEW)
+        if t == quarter:
+            line_ready(0)
             unit(0, 0, y, 0, half)
-        elif t == 3:
-            for u in (0, 1):
-                sib_side(u)
+        elif t == quarter + 1:
+            side_ready(0)
             unit(0, 0, 1 - y, 0, half)
-        elif t == 4:
+        elif t == 2 * quarter:
             set_rows(1, partner)
-            for u in (2, 3):
-                sib_line(u)
+            line_ready(1)
             unit(1, 0, y, 0, rows)
-        elif t == 5:
-            for u in (2, 3):
-                sib_side(u)
-            unit(1, 0, 1 - y, 0, rows)
-        elif t == 6:
-            for u in (4, 5):
-                sib_line(u)
+        elif t == 2 * quarter + 1:
+            unit(1, 0, 1 - y, 0, half)
+        elif t == 2 * quarter + 2:
+            line_ready(2)
             unit(1, 1, y, 0, half)
-            unit(0, 0, y, half, half)
-        elif t == 7:
-            for u in (4, 5):
-                sib_side(u)
-            unit(1, 1, 1 - y, 0, half)
-            for u in (6, 7):
-                sib_line(u)
-            unit(1, 1, y, half, half)
+        elif t == 2 * quarter + 3:
+            side_ready(1)
+            unit(1, 0, 1 - y, half, half)
+    from_side(2 * CHUNKS - 2)
+    line_ready(3)
+    unit(1, 1, y, half, half)
+    side_ready(2)
+    unit(1, 1, 1 - y, 0, half)
     from_side(2 * CHUNKS - 1)
-    for u in (6, 7):
-        sib_side(u)
+    side_ready(3)
     unit(1, 1, 1 - y, half, half)
 
     for piece in range(PARTS):
@@ -233,6 +244,7 @@
         res_out[at, :feat] = (acc_grad[1, at, :] - total * x).astype(jnp.bfloat16)
         result(piece).start()
 
+    unit(0, 0, y, half, half)
     unit(0, 0, 1 - y, half, half)
     unit(0, 1, y, 0, rows)
     unit(0, 1, 1 - y, 0, rows)
@@ -262,8 +274,8 @@
     @pl.when(inner)
     def _():
         for chunk in range(CHUNKS):
-            copy(me, chunk, send_mid.at[chunk], mid).wait_send()
-            copy(partner, chunk, send_mid.at[CHUNKS + chunk], mid).wait_send()
+            to_mid(chunk).wait_send()
+            to_mid(CHUNKS + chunk).wait_send()
 
 
 def paired_device(depth, points, left, right):

time: 47.3 us -> 45.3 us (0.958)
  Pallas kernels: 43.8 us -> 41.8 us
    pallas_call x1, Pallas kernels: 43.8 us -> 41.8 us  [paired_device(): pl.pallas_call(functools.partial(paired_kernel, depth), out_shape=(jax.Sh...]
where the time goes in v3:
time: 45.3 us; the launch traced here: 45.1 us
  Pallas kernels  41.8 us (92%)
  local copies, waits for them, and re-layouts  2.62 us (6%)
  between operations  0.68 us (2%)
    pallas_call x1, Pallas kernels, paired_device(): pl.pallas_call(functools.partial(paired_kernel, depth), out_shape=(jax.Sh...  41.8 us
    unnamed x8, local copies, waits for them, and re-layouts  2.62 us

profile of v3, /device:TPU:0, one launch (start us, length us, event | category | flops | bytes accessed | tf_op | source)
XLA Modules:
  0.0 45.1 jit_solution(11084682489428122883)
XLA Ops:
  0.6 0.0 copy-start.1
  0.6 0.0 copy-start
  0.6 1.0 %copy.5.left = bf16[512,64]{1,0:T(8,128)(2,1)S(1)} copy(bf16[512,64]{0,1:T(8,128)(2,1)} %param.4) | data formatting | bytes 131072 | tf_op args[1]
  1.7 0.0 copy-done.1
  1.7 0.1 copy.6.right
  1.8 0.0 copy-done
  1.8 41.8 %shard_map.50 = (f32[512,128]{1,0:T(8,128)S(1)}, f32[512,256]{1,0:T(8,128)S(1)}) custom-call(bf16[512,256]{1,0:T(8,128)(2,1)S(1)} %copy-done, bf16[512,64]{1,0:T(8,128)(2,1)S(1)} %copy.5.left, bf16[512,64]{1,0:T(8,128)(2,1)S(1)} %copy.6.right), custom_call_target="tpu_custom_call" | custom-call | tf_op jit(solution)/shard_map/pallas_call | solution.py:286
  43.6 0.7 %copy.9 = f32[512,128]{1,0:T(8,128)} copy(f32[512,128]{1,0:T(8,128)S(1)} %get-tuple-element.4) | data formatting | bytes 524288
  44.3 0.8 %copy.10 = f32[512,256]{1,0:T(8,128)} copy(f32[512,256]{1,0:T(8,128)S(1)} %get-tuple-element.5) | data formatting | bytes 1048576
Async XLA Ops:
  0.6 1.0 %copy-start.1 = (bf16[512,64]{0,1:T(8,128)(2,1)S(1)}, bf16[512,64]{0,1:T(8,128)(2,1)}, u32[]{:S(2)}) copy-start(bf16[512,64]{0,1:T(8,128)(2,1)} %param.5) | copy-start | bytes 196612
  0.6 1.2 %copy-start = (bf16[512,256]{1,0:T(8,128)(2,1)S(1)}, bf16[512,256]{1,0:T(8,128)(2,1)}, u32[]{:S(2)}) copy-start(bf16[512,256]{1,0:T(8,128)(2,1)} %points.1) | copy-start | bytes 786436

commit v4 on v3

--- a/solution.py
+++ b/solution.py
@@ -10,7 +10,7 @@
 
 MESH = pl.DeviceIdType.MESH
 CHUNKS = 4
-WINDOW = 3
+WINDOW = 4
 SKEW = 2
 PARTS = 4
 NT = (((1,), (1,)), ((), ()))
@@ -125,16 +125,14 @@
     acc_grad[...] = jnp.zeros_like(acc_grad)
     acc_sum[...] = jnp.zeros_like(acc_sum)
 
-    strip = rows
-
-    def unit(which, order, yy, begin, length):
+    def unit(which, order, yy, begin, length, pieces=((0, rows),)):
         first_slot = slot_of(first if order == 0 else second, yy, 0)
         span = pl.ds(begin, length)
         cols_x = blocks[pl.ds(first_slot, 2), span, :feat].reshape(2 * length, feat)
         cols_right = blocks[pl.ds(first_slot, 2), span, feat:].reshape(2 * length, -1)
         cols_sq = column_squares(cols_x) * half_log
         row_slot = partner if which else me
-        for at in range(0, rows, strip):
+        for at, strip in pieces:
             here = pl.ds(at, strip)
             sq = squares[which, here, :]
             vu, grad, sums = pair_block(
@@ -233,10 +231,9 @@
     unit(1, 1, 1 - y, 0, half)
     from_side(2 * CHUNKS - 1)
     side_ready(3)
-    unit(1, 1, 1 - y, half, half)
-
+    span = rows // PARTS
     for piece in range(PARTS):
-        span = rows // PARTS
+        unit(1, 1, 1 - y, half, half, ((piece * span, span),))
         at = pl.ds(piece * span, span)
         total = jnp.sum(acc_sum[1, at, :], axis=1, keepdims=True)
         x = blocks[partner, at, :feat].astype(jnp.float32)
@@ -255,10 +252,13 @@
         at = pl.ds(piece * span, span)
         total = jnp.sum(acc_sum[0, at, :], axis=1, keepdims=True)
         x = blocks[me, at, :feat].astype(jnp.float32)
-        grad = acc_grad[0, at, :] - total * x
+        out_vu[at, :] = acc_vu[0, at, :] * scale
+        out_grad[at, :] = (acc_grad[0, at, :] - total * x) * scale
+    for piece in range(PARTS):
+        at = pl.ds(piece * span, span)
         result(piece).wait_recv()
-        out_vu[at, :] = (acc_vu[0, at, :] + res_in[at, feat:].astype(jnp.float32)) * scale
-        out_grad[at, :] = (grad + res_in[at, :feat].astype(jnp.float32)) * scale
+        out_vu[at, :] += res_in[at, feat:].astype(jnp.float32) * scale
+        out_grad[at, :] += res_in[at, :feat].astype(jnp.float32) * scale
 
     for piece in range(PARTS):
         result(piece).wait_send()

time: 45.3 us -> 44.8 us (0.989)
  no operation moved by 1% of the time
where the time goes in v4:
time: 44.8 us; the launch traced here: 44.7 us
  Pallas kernels  41.4 us (92%)
  local copies, waits for them, and re-layouts  2.62 us (6%)
  between operations  0.68 us (2%)
    pallas_call x1, Pallas kernels, paired_device(): pl.pallas_call(functools.partial(paired_kernel, depth), out_shape=(jax.Sh...  41.4 us
    unnamed x8, local copies, waits for them, and re-layouts  2.62 us

profile of v4, /device:TPU:0, one launch (start us, length us, event | category | flops | bytes accessed | tf_op | source)
XLA Modules:
  0.0 44.7 jit_solution(1107615358490579158)
XLA Ops:
  0.6 0.0 copy-start.1
  0.6 0.0 copy-start
  0.6 1.0 %copy.5.left = bf16[512,64]{1,0:T(8,128)(2,1)S(1)} copy(bf16[512,64]{0,1:T(8,128)(2,1)} %param.4) | data formatting | bytes 131072 | tf_op args[1]
  1.7 0.0 copy-done.1
  1.7 0.1 copy.6.right
  1.8 0.0 copy-done
  1.8 41.4 %shard_map.50 = (f32[512,128]{1,0:T(8,128)S(1)}, f32[512,256]{1,0:T(8,128)S(1)}) custom-call(bf16[512,256]{1,0:T(8,128)(2,1)S(1)} %copy-done, bf16[512,64]{1,0:T(8,128)(2,1)S(1)} %copy.5.left, bf16[512,64]{1,0:T(8,128)(2,1)S(1)} %copy.6.right), custom_call_target="tpu_custom_call" | custom-call | tf_op jit(solution)/shard_map/pallas_call | solution.py:286
  43.2 0.7 %copy.9 = f32[512,128]{1,0:T(8,128)} copy(f32[512,128]{1,0:T(8,128)S(1)} %get-tuple-element.4) | data formatting | bytes 524288
  43.9 0.8 %copy.10 = f32[512,256]{1,0:T(8,128)} copy(f32[512,256]{1,0:T(8,128)S(1)} %get-tuple-element.5) | data formatting | bytes 1048576
Async XLA Ops:
  0.6 1.0 %copy-start.1 = (bf16[512,64]{0,1:T(8,128)(2,1)S(1)}, bf16[512,64]{0,1:T(8,128)(2,1)}, u32[]{:S(2)}) copy-start(bf16[512,64]{0,1:T(8,128)(2,1)} %param.5) | copy-start | bytes 196612
  0.6 1.2 %copy-start = (bf16[512,256]{1,0:T(8,128)(2,1)S(1)}, bf16[512,256]{1,0:T(8,128)(2,1)}, u32[]{:S(2)}) copy-start(bf16[512,256]{1,0:T(8,128)(2,1)} %points.1) | copy-start | bytes 786436
